TPU v7x, 256 devices: a whole 4x4x8 slice. The times are simulated.
256 devices in a mesh: grp: 4 (over x), dev: 64 (over y, z, core).
Axes of the slice: x: 4, y: 4, z: 8, core: 2. Of those that a mesh axis runs over, the one named last changes fastest.
Arguments:
- nodes: bfloat16 [98304, 512], P(('grp', 'dev')), may hold values from -6 to 6
- senders: int32 [589824], P(('grp', 'dev')), may hold values from 0 to 1151
- mid_nodes: bfloat16 [24576, 512], P(('grp', 'dev')), may hold values from -6 to 6
- owners: int32 [98304, 1], P(('grp', 'dev')), may hold values from 0 to 63; in each aligned block of 384 rows (0 to 383, 384 to 767, ...) at most 12 rows name the same one
- slots: int32 [98304], P(('grp', 'dev')), may hold values from 0 to 95
- edge_in: bfloat16 [1024, 512], replicated, may hold values from -0.1875 to 0.1875
- edge_out: bfloat16 [512, 512], replicated, may hold values from -0.25 to 0.25
- node_in: bfloat16 [1024, 512], replicated, may hold values from -0.1875 to 0.1875
- node_out: bfloat16 [512, 512], replicated, may hold values from -0.25 to 0.25
- up_weight: bfloat16 [512, 512], replicated, may hold values from -0.25 to 0.25
- mid_in: bfloat16 [1024, 512], replicated, may hold values from -0.1875 to 0.1875
- mid_out: bfloat16 [512, 512], replicated, may hold values from -0.25 to 0.25
- down_in: bfloat16 [1024, 512], replicated, may hold values from -0.1875 to 0.1875
Outputs:
- fine_out: bfloat16 [98304, 512], P(('grp', 'dev'))
- mid_new: bfloat16 [24576, 512], P(('grp', 'dev'))
Inputs may be any that keep to these rules, and one draw needn't show every extreme that they name: `owners`: among the 384 fine nodes of one device, at most 12 name the same owner value, a bound that some block reaches.
All inputs are finite; a program needn't handle non-finite values.
Results may differ from a plain program's by a relative error of at most 0.014.
Values may be sent and summed in bfloat16 or wider, within the bound.
A program may use at most 64 MiB of HBM per device.

v0:
```python
import jax
import jax.numpy as jnp
from jax import lax
from jax.sharding import Mesh
from jax.sharding import PartitionSpec as P

GRP_DEV = ("grp", "dev_0", "dev_1", "dev_2")
DEV = ("dev_0", "dev_1", "dev_2")


def padded(value, sides, width):
    edges = {}
    for axis, dim in sides:
        size, length = (lax.axis_size(axis), value.shape[dim])
        up = [(i, (i + 1) % size) for i in range(size)]
        last = lax.slice_in_dim(value, length - width, length, axis=dim)
        initial = lax.slice_in_dim(value, 0, width, axis=dim)
        edges[dim] = (
            lax.ppermute(last, axis, up),
            lax.ppermute(initial, axis, [(b, a) for a, b in up]),
        )
    done = []
    for _, dim in sides:
        low, high = edges[dim]
        around = [(width, width) if d in done else (0, 0) for d in range(value.ndim)]
        value = jnp.concatenate([jnp.pad(low, around), value, jnp.pad(high, around)], axis=dim)
        done.append(dim)
    return value


def in_blocks(value, dim, size):
    shape = value.shape
    tiles = value.reshape(*shape[:dim], size, shape[dim] // size, *shape[dim + 1 :])
    return jnp.moveaxis(tiles, dim, 0)


def joined_along(tiles, dim):
    tiles = jnp.moveaxis(tiles, 0, dim)
    shape = tiles.shape
    return tiles.reshape(*shape[:dim], shape[dim] * shape[dim + 1], *shape[dim + 2 :])


def exchange_in_order(tiles, axes, turns):
    shape = [lax.axis_size(a) for a in axes]
    tiles = tiles.reshape(*shape, *tiles.shape[1:])
    for k in turns:
        tiles = lax.all_to_all(tiles, axes[k], split_axis=k, concat_axis=k, tiled=True)
    return tiles.reshape(-1, *tiles.shape[len(axes) :])


def two_step_exchange(value, groups, turns, split_dim, concat_dim):
    size = lax.axis_size(groups[0]) * lax.axis_size(groups[1])
    tiles = in_blocks(value, split_dim, size)
    return joined_along(exchange_in_order(tiles, groups, turns), concat_dim)


def coarse_update(mid_nodes, up_sum, mid_in, mid_out):
    joined = jnp.concatenate([mid_nodes, up_sum], axis=1)
    mid_hidden = jax.nn.silu(jnp.dot(joined, mid_in, preferred_element_type=jnp.float32)).astype(
        jnp.bfloat16
    )
    return (
        mid_nodes.astype(jnp.float32)
        + jnp.dot(mid_hidden, mid_out, preferred_element_type=jnp.float32)
    ).astype(jnp.bfloat16)


def one_hot_rows(wanted, count):
    columns = jnp.arange(count, dtype=jnp.int32)
    return (wanted[:, None] == columns[None, :]).astype(jnp.bfloat16)


def body(
    nodes,
    senders,
    mid_nodes,
    owners,
    slots,
    edge_in,
    edge_out,
    node_in,
    node_out,
    up_weight,
    mid_in,
    mid_out,
    down_in,
):
    row_count = nodes.shape[0]
    feat_width = nodes.shape[1]
    degree = senders.shape[0] // row_count
    extended = padded(nodes, ((GRP_DEV, 0),), row_count)
    picker = one_hot_rows(senders, extended.shape[0])
    src_rows = jnp.dot(picker, extended, preferred_element_type=jnp.float32).astype(jnp.bfloat16)
    src_proj = jnp.dot(src_rows, edge_in[:feat_width], preferred_element_type=jnp.float32)
    dst_proj = jnp.dot(nodes, edge_in[feat_width:], preferred_element_type=jnp.float32)
    edge_pre = src_proj.reshape(row_count, degree, feat_width) + dst_proj[:, None, :]
    edge_hidden = jax.nn.silu(edge_pre).astype(jnp.bfloat16).reshape(row_count * degree, feat_width)
    edge_msg = jnp.dot(edge_hidden, edge_out, preferred_element_type=jnp.float32).astype(
        jnp.bfloat16
    )
    agg = (
        edge_msg.astype(jnp.float32)
        .reshape(row_count, degree, feat_width)
        .sum(axis=1)
        .astype(jnp.bfloat16)
    )
    node_hidden = jax.nn.silu(
        jnp.dot(jnp.concatenate([nodes, agg], axis=1), node_in, preferred_element_type=jnp.float32)
    ).astype(jnp.bfloat16)
    fine_new = (
        nodes.astype(jnp.float32)
        + jnp.dot(node_hidden, node_out, preferred_element_type=jnp.float32)
    ).astype(jnp.bfloat16)
    up_msg = jax.nn.silu(jnp.dot(fine_new, up_weight, preferred_element_type=jnp.float32)).astype(
        jnp.bfloat16
    )
    owner_ids = owners[:, 0]
    mid_rows = mid_nodes.shape[0]
    peer_count = lax.axis_size(DEV)
    capacity = max(2, 2 * row_count // peer_count)
    owner_hot = (owner_ids[:, None] == jnp.arange(peer_count, dtype=jnp.int32)[None, :]).astype(
        jnp.bfloat16
    )
    row_pos = jnp.arange(row_count, dtype=jnp.int32)
    earlier = (row_pos[None, :] < row_pos[:, None]).astype(jnp.bfloat16)
    before_counts = jnp.dot(earlier, owner_hot, preferred_element_type=jnp.float32)
    rank_ids = jnp.sum(before_counts * owner_hot.astype(jnp.float32), axis=1).astype(jnp.int32)
    flat_ids = owner_ids * capacity + rank_ids
    placing = one_hot_rows(flat_ids, peer_count * capacity)
    placing_t = placing.T
    send_rows = jnp.dot(placing_t, up_msg, preferred_element_type=jnp.float32).astype(jnp.bfloat16)
    filled = jnp.sum(placing_t.astype(jnp.float32), axis=1)
    slot_vals = jnp.dot(placing_t.astype(jnp.float32), slots.astype(jnp.float32)[:, None])[:, 0]
    send_slots = jnp.where(filled > 0.5, slot_vals, float(mid_rows)).astype(jnp.int32)
    send_rows = send_rows.reshape(peer_count, capacity, feat_width)
    send_slots = send_slots.reshape(peer_count, capacity)
    got_rows, got_slots = (
        lax.all_to_all(send_rows, DEV, split_axis=0, concat_axis=0, tiled=True),
        lax.all_to_all(send_slots, DEV, split_axis=0, concat_axis=0, tiled=True),
    )
    flat_slots = got_slots.reshape(-1)
    slot_hot = one_hot_rows(flat_slots, mid_rows)
    up_sum = jnp.dot(
        slot_hot.T, got_rows.reshape(-1, feat_width), preferred_element_type=jnp.float32
    ).astype(jnp.bfloat16)
    mid_new = coarse_update(mid_nodes, up_sum, mid_in, mid_out)
    back_rows = jnp.dot(slot_hot, mid_new, preferred_element_type=jnp.float32).astype(jnp.bfloat16)
    back_rows = back_rows.reshape(peer_count, capacity, feat_width)
    returned = two_step_exchange(back_rows, (("dev_0", "dev_1"), "dev_2"), (1, 0), 0, 0)
    parent_rows = jnp.dot(
        placing, returned.reshape(-1, feat_width), preferred_element_type=jnp.float32
    ).astype(jnp.bfloat16)
    downward = jax.nn.silu(
        jnp.dot(
            jnp.concatenate([fine_new, parent_rows], axis=1),
            down_in,
            preferred_element_type=jnp.float32,
        )
    )
    fine_out = (fine_new.astype(jnp.float32) + downward).astype(jnp.bfloat16)
    return (fine_out, mid_new)


def solution(mesh):
    split = Mesh(
        mesh.devices.reshape(mesh.shape["grp"], 4, 8, 2), ("grp", "dev_0", "dev_1", "dev_2")
    )
    in_specs = (
        P(GRP_DEV, None),
        P(GRP_DEV),
        P(GRP_DEV, None),
        P(GRP_DEV, None),
        P(GRP_DEV),
        P(),
        P(),
        P(),
        P(),
        P(),
        P(),
        P(),
        P(),
    )
    out_specs = (P(GRP_DEV, None), P(GRP_DEV, None))
    return jax.shard_map(body, mesh=split, in_specs=in_specs, out_specs=out_specs, check_vma=False)
```

profile of v0, /device:TPU:38, one launch (start us, length us, event | category | flops | bytes accessed | tf_op | source)
XLA Modules:
  0.0 134.6 jit_solution(11399013599467937666)
XLA Ops:
  1.2 0.7 reduce.1
  2.2 0.7 add_reduce_fusion
  2.9 0.7 convert_element_type.114
  4.1 0.7 convert_element_type.116
  4.9 16.4 %all-to-all-start = ((s32[64,1,12]{2,1,0:T(1,128)}), s32[64,1,12]{2,1,0:T(1,128)S(1)}, u32[]{:S(2)}, u32[]{:S(2)}) async-start(s32[64,1,12]{2,1,0:T(1,128)} %bitcast), calls=%async_computation | async-start | bytes 65536 | tf_op jit(solution)/shard_map/all_to_all | solution.py:139
  21.2 1.5 %fusion.36 = f32[384,512]{1,0:T(8,128)S(1)} fusion(bf16[384,512]{1,0:T(8,128)(2,1)} %param.13, bf16[1024,512]{1,0:T(8,128)(2,1)} %param.18), kind=kOutput, calls=%fused_computation.43 | convolution fusion | flops 201326592 | bytes 1703936 | tf_op jit(solution)/shard_map/dot_general | solution.py:95
  22.7 3.5 %add.43 = f32[384,6,512]{2,1,0:T(8,128)} broadcast(f32[384,512]{1,0:T(8,128)S(1)} %fusion.36), dimensions={0,2} | broadcast | bytes 5505024 | tf_op jit(solution)/shard_map/add | solution.py:96
  26.2 6.9 %add.44 = f32[2304,512]{1,0:T(8,128)} reshape(f32[384,6,512]{2,1,0:T(8,128)} %add.43) | data formatting | bytes 9437184 | tf_op jit(solution)/shard_map/add | solution.py:96
  33.1 8.4 %multiply_convert_fusion = bf16[2304,512]{1,0:T(8,128)(2,1)} fusion(f32[2304,512]{1,0:T(8,128)} %add.44, s32[2304]{0:T(1024)S(1)} %copy-done.9, bf16[384,512]{1,0:T(8,128)(2,1)S(1)} %collective-permute-done.1, bf16[384,512]{1,0:T(8,128)(2,1)S(1)} %copy-done.1, bf16[384,512]{1,0:T(8,128)(2,1)S(1)} %collective-permute-done, bf16[1024,512]{1,0:T(8,128)(2,1)S(1)} %copy-done.3), kind=kOutput, calls=%fused_computation.4 | convolution fusion | flops 3940319232 | bytes 8794112 | tf_op jit(solution)/shard_map/dot_general | solution.py:94
  41.5 3.1 %convolution_convert_fusion = bf16[2304,512]{1,0:T(8,128)(2,1)S(1)} fusion(bf16[2304,512]{1,0:T(8,128)(2,1)} %multiply_convert_fusion, bf16[512,512]{1,0:T(8,128)(2,1)} %param.19), kind=kOutput, calls=%fused_computation.6 | convolution fusion | flops 1209139200 | bytes 5242880 | tf_op jit(solution)/shard_map/dot_general | solution.py:98
  44.7 2.5 %reshape.68 = bf16[384,6,512]{2,1,0:T(8,128)(2,1)} reshape(bf16[2304,512]{1,0:T(8,128)(2,1)S(1)} %convolution_convert_fusion) | data formatting | bytes 4718592 | tf_op jit(solution)/shard_map/reshape | solution.py:103
  47.1 3.9 %reduce = bf16[384,512]{1,0:T(8,128)(2,1)S(1)} reduce(bf16[384,6,512]{2,1,0:T(8,128)(2,1)} %reshape.68, bf16[]{:T(256)} %constant.22), dimensions={1}, to_apply=%region_0.1.clone | reduce | flops 983040 | bytes 2752514 | tf_op jit(solution)/shard_map/reduce_sum | solution.py:104
  51.0 0.9 fusion.3
  52.1 1.0 convolution_convert_fusion.2
  53.1 1.2 reshape.70
  54.2 10.6 %all-to-all-start.1 = ((bf16[64,12,512]{2,1,0:T(8,128)(2,1)}), bf16[64,12,512]{2,1,0:T(8,128)(2,1)S(1)}, u32[]{:S(2)}, u32[]{:S(2)}) async-start(bf16[64,12,512]{2,1,0:T(8,128)(2,1)} %reshape.70), calls=%async_computation.1 | async-start | bytes 2097152 | tf_op jit(solution)/shard_map/all_to_all | solution.py:138
  64.9 0.5 broadcast.42
  65.4 0.7 reduce.9
  66.2 26.5 %all-to-all-done.1 = bf16[64,12,512]{2,1,0:T(8,128)(2,1)S(1)} async-done(((bf16[64,12,512]{2,1,0:T(8,128)(2,1)}), bf16[64,12,512]{2,1,0:T(8,128)(2,1)S(1)}, u32[]{:S(2)}, u32[]{:S(2)}) %all-to-all-start.1) | async-done | bytes 786464 | tf_op jit(solution)/shard_map/all_to_all | solution.py:138
  93.4 1.7 %fusion.16 = bf16[96,512]{1,0:T(8,128)(2,1)S(1)} fusion(bf16[512,512]{1,0:T(8,128)(2,1)S(1)} %copy-done.7, bf16[1024,512]{1,0:T(8,128)(2,1)} %param.23, bf16[96,512]{1,0:T(8,128)(2,1)S(1)} %convolution_convert_fusion.4, bf16[96,512]{1,0:T(8,128)(2,1)S(1)} %copy-done.8), kind=kOutput, calls=%fused_computation.23 | convolution fusion | flops 151781376 | bytes 1867776 | tf_op jit(solution)/shard_map/dot_general | solution.py:64
  96.2 4.4 %all_to_all.21 = bf16[32,2,1,12,512]{4,0,3,2,1:T(8,128)(2,1)S(1)} all-to-all(bf16[32,2,1,12,512]{4,0,3,2,1:T(8,128)(2,1)S(1)} %copy.20), channel_id=1, replica_groups=mesh['grp'=4,'dev_0'=4,'dev_1'=8,'dev_2'=2] {'dev_2'}, dimensions={1} | all-to-all | bytes 1572864 | tf_op jit(solution)/shard_map/all_to_all | solution.py:47
  100.6 0.8 copy.21
  101.4 29.6 %all_to_all.22 = bf16[32,2,1,12,512]{4,1,3,2,0:T(2,128)(2,1)S(1)} all-to-all(bf16[32,2,1,12,512]{4,1,3,2,0:T(2,128)(2,1)S(1)} %copy.21), channel_id=1, replica_groups=mesh['grp'=4,'dev_0'=4,'dev_1'=8,'dev_2'=2] {'dev_0','dev_1'}, dimensions={0} | all-to-all | bytes 1572864 | tf_op jit(solution)/shard_map/all_to_all | solution.py:47
  131.9 2.7 %add_convert_fusion = bf16[384,512]{1,0:T(8,128)(2,1)} fusion(bf16[1024,512]{1,0:T(8,128)(2,1)} %param.25, bf16[384,512]{1,0:T(8,128)(2,1)S(1)} %convolution_convert_fusion.3, bf16[384,512]{1,0:T(8,128)(2,1)S(1)} %copy-done.11), kind=kOutput, calls=%fused_computation.36 | convolution fusion | flops 405602304 | bytes 2228224 | tf_op jit(solution)/shard_map/dot_general | solution.py:154
  (44 shorter events, 4.3 us)
Async XLA Ops:
  0.6 50.4 %copy-start = (bf16[1024,512]{1,0:T(8,128)(2,1)S(1)}, bf16[1024,512]{1,0:T(8,128)(2,1)}, u32[]{:S(2)}) copy-start(bf16[1024,512]{1,0:T(8,128)(2,1)} %param.20) | copy-start | bytes 3145732
  0.6 32.5 %collective-permute-start.1 = (bf16[384,512]{1,0:T(8,128)(2,1)}, bf16[384,512]{1,0:T(8,128)(2,1)S(1)}, u32[]{:S(2)}, u32[]{:S(2)}) collective-permute-start(bf16[384,512]{1,0:T(8,128)(2,1)} %param.13), channel_id=1, source_target_pairs={{1,0},{2,1},{3,2},{4,3},{5,4},{6,5},{7,6},{8,7},{9,8},{10,9},{11,1... | collective-permute-start | bytes 1179656 | tf_op jit(solution)/shard_map/ppermute | solution.py:20
  0.7 32.4 %collective-permute-start = (bf16[384,512]{1,0:T(8,128)(2,1)}, bf16[384,512]{1,0:T(8,128)(2,1)S(1)}, u32[]{:S(2)}, u32[]{:S(2)}) collective-permute-start(bf16[384,512]{1,0:T(8,128)(2,1)} %param.13), channel_id=1, source_target_pairs={{0,1},{1,2},{2,3},{3,4},{4,5},{5,6},{6,7},{7,8},{8,9},{9,10},{10,1... | collective-permute-start | bytes 1179656 | tf_op jit(solution)/shard_map/ppermute | solution.py:19
  4.9 49.4 %all-to-all-start = ((s32[64,1,12]{2,1,0:T(1,128)}), s32[64,1,12]{2,1,0:T(1,128)S(1)}, u32[]{:S(2)}, u32[]{:S(2)}) async-start(s32[64,1,12]{2,1,0:T(1,128)} %bitcast), calls=%async_computation | async-start | bytes 65536 | tf_op jit(solution)/shard_map/all_to_all | solution.py:139
  26.2 6.9 %copy-start.1 = (bf16[384,512]{1,0:T(8,128)(2,1)S(1)}, bf16[384,512]{1,0:T(8,128)(2,1)}, u32[]{:S(2)}) copy-start(bf16[384,512]{1,0:T(8,128)(2,1)} %param.13) | copy-start | bytes 1179652
  26.2 6.9 %copy-start.3 = (bf16[1024,512]{1,0:T(8,128)(2,1)S(1)}, bf16[1024,512]{1,0:T(8,128)(2,1)}, u32[]{:S(2)}) copy-start(bf16[1024,512]{1,0:T(8,128)(2,1)} %param.18) | copy-start | bytes 3145732
  26.2 6.9 %copy-start.9 = (s32[2304]{0:T(1024)S(1)}, s32[2304]{0:T(1024)}, u32[]{:S(2)}) copy-start(s32[2304]{0:T(1024)} %param.14) | copy-start | bytes 27652
  47.1 3.9 %copy-start.2 = (bf16[384,512]{1,0:T(8,128)(2,1)S(1)}, bf16[384,512]{1,0:T(8,128)(2,1)}, u32[]{:S(2)}) copy-start(bf16[384,512]{1,0:T(8,128)(2,1)} %param.13) | copy-start | bytes 1179652
  47.1 3.9 %copy-start.5 = (bf16[512,512]{1,0:T(8,128)(2,1)S(1)}, bf16[512,512]{1,0:T(8,128)(2,1)}, u32[]{:S(2)}) copy-start(bf16[512,512]{1,0:T(8,128)(2,1)} %param.21) | copy-start | bytes 1572868
  51.0 1.0 copy-start.6
  52.1 1.0 copy-start.10
  54.2 39.2 %copy-start.7 = (bf16[512,512]{1,0:T(8,128)(2,1)S(1)}, bf16[512,512]{1,0:T(8,128)(2,1)}, u32[]{:S(2)}) copy-start(bf16[512,512]{1,0:T(8,128)(2,1)} %param.24) | copy-start | bytes 1572868
  54.2 39.2 %copy-start.8 = (bf16[96,512]{1,0:T(8,128)(2,1)S(1)}, bf16[96,512]{1,0:T(8,128)(2,1)}, u32[]{:S(2)}) copy-start(bf16[96,512]{1,0:T(8,128)(2,1)} %param.15) | copy-start | bytes 294916
  54.2 38.5 %all-to-all-start.1 = ((bf16[64,12,512]{2,1,0:T(8,128)(2,1)}), bf16[64,12,512]{2,1,0:T(8,128)(2,1)S(1)}, u32[]{:S(2)}, u32[]{:S(2)}) async-start(bf16[64,12,512]{2,1,0:T(8,128)(2,1)} %reshape.70), calls=%async_computation.1 | async-start | bytes 2097152 | tf_op jit(solution)/shard_map/all_to_all | solution.py:138
  95.1 5.4 %copy-start.4 = (bf16[96,512]{1,0:T(8,128)(2,1)}, bf16[96,512]{1,0:T(8,128)(2,1)S(1)}, u32[]{:S(2)}) copy-start(bf16[96,512]{1,0:T(8,128)(2,1)S(1)} %fusion.16) | copy-start | bytes 294916
  130.9 1.0 copy-start.11
where the time goes:
time: 135 us
  blocking collectives  33.9 us (25%)
  starting transfers between devices  27.6 us (20%)
  waiting for transfers between devices  26.5 us (20%)
  matrix products  21.3 us (16%)
  local copies, waits for them, and re-layouts  17.5 us (13%)
  other arithmetic  6.9 us (5%)
    all_to_all x2, blocking collectives, exchange_in_order(): lax.all_to_all(tiles, axes[k], split_axis=k, concat_axis=k, tiled=True)  33.9 us
    all_to_all x1, waiting for transfers between devices, body(): lax.all_to_all(send_rows, DEV, split_axis=0, concat_axis=0, tiled=True)  26.5 us
    all_to_all x1, starting transfers between devices, body(): lax.all_to_all(send_slots, DEV, split_axis=0, concat_axis=0, tiled=True)  16.4 us
    all_to_all x1, starting transfers between devices, body(): lax.all_to_all(send_rows, DEV, split_axis=0, concat_axis=0, tiled=True)  10.6 us
    add x2, local copies, waits for them, and re-layouts, body(): src_proj.reshape(row_count, degree, feat_width) + dst_proj[:, None, :]  10.3 us
    dot_general x1, matrix products, body(): jnp.dot(src_rows, edge_in[:feat_width], preferred_element_type=jnp.float32)  8.4 us
    reduce_sum x1, other arithmetic, body(): agg = edge_msg.astype(jnp.float32).reshape(row_count, degree, feat_width)...  3.87 us
    dot_general x1, matrix products, body(): jnp.dot(edge_hidden, edge_out, preferred_element_type=jnp.float32)  3.13 us
  transfers between devices with their start and end apart: 4, of which 1 were waited for; matrix products, arithmetic and copies ran while one was open for 28% of the time, Pallas kernels for 0%

commit v1 on v0

v1 whole, which is shorter than its diff:
```python
import functools

import jax
import jax.numpy as jnp
from jax import lax
from jax.experimental import pallas as pl
from jax.experimental.pallas import tpu as pltpu
from jax.sharding import PartitionSpec as P

MESH = pl.DeviceIdType.MESH
BOTH = ("grp", "dev")
BF = jnp.bfloat16
F32 = jnp.float32


def silu(x):
    half = 0.5 * x
    return half + half * jnp.tanh(half)


def mm(a, b):
    return jnp.dot(a, b, preferred_element_type=F32)


def hot(match):
    return jnp.where(match, 1.0, 0.0).astype(BF)


def swap4(x):
    return pltpu.roll(x, 4, 1)


def pack(rows, pairs):
    groups = rows.shape[0] // 8
    t = [rows[:, 128 * j : 128 * (j + 1)].reshape(groups, 8, 128) for j in range(4)]
    low = lax.broadcasted_iota(jnp.int32, (groups, 8, 128), 1) < 4
    first = [jnp.where(low, t[j], swap4(t[j + 1])) for j in (0, 2)]
    second = [jnp.where(low, swap4(t[j]), t[j + 1]) for j in (0, 2)]
    first = jnp.concatenate(first, axis=1).astype(BF).reshape(pairs, 1, 3, 16, 128)
    second = jnp.concatenate(second, axis=1).astype(BF).reshape(pairs, 1, 3, 16, 128)
    return jnp.concatenate([first, second], axis=1).reshape(2 * pairs, 3, 16, 128)


def unpack(blocks, pairs):
    both = blocks.astype(F32).reshape(pairs, 2, 3, 16, 128)
    first = both[:, 0].reshape(pairs * 3, 16, 128)
    second = both[:, 1].reshape(pairs * 3, 16, 128)
    low = lax.broadcasted_iota(jnp.int32, (pairs * 3, 8, 128), 1) < 4
    tiles = []
    for half in (slice(0, 8), slice(8, 16)):
        a, b = first[:, half], second[:, half]
        tiles.append(jnp.where(low, a, swap4(b)).reshape(pairs * 24, 128).astype(BF))
        tiles.append(jnp.where(low, swap4(a), b).reshape(pairs * 24, 128).astype(BF))
    return jnp.concatenate(tiles, axis=1)


def pack_hot(rows, pairs):
    g = rows.reshape(pairs, 3, 8, 128)
    g0, g1, g2 = g[:, 0], g[:, 1], g[:, 2]
    low = lax.broadcasted_iota(jnp.int32, (pairs, 8, 128), 1) < 4
    first = jnp.concatenate([jnp.where(low, g0, swap4(g1)), g2], axis=1).astype(BF)
    second = jnp.concatenate([jnp.where(low, swap4(g0), g1), swap4(g2)], axis=1).astype(BF)
    out = jnp.concatenate([first.reshape(pairs, 1, 16, 128), second.reshape(pairs, 1, 16, 128)], axis=1)
    return out.reshape(2 * pairs, 16, 128)


def unpack_hot(blocks, pairs):
    both = blocks.astype(F32).reshape(pairs, 2, 16, 128)
    a, b = both[:, 0], both[:, 1]
    low = lax.broadcasted_iota(jnp.int32, (pairs, 8, 128), 1) < 4
    u0 = jnp.where(low, a[:, 0:8], swap4(b[:, 0:8]))
    u1 = jnp.where(low, swap4(a[:, 0:8]), b[:, 0:8])
    u2 = jnp.where(low, a[:, 8:16], swap4(b[:, 8:16]))
    return jnp.concatenate([u[:, None] for u in (u0, u1, u2)], axis=1).reshape(pairs * 24, 128)


def kernel(
    n_grp, n_dev,
    ints_ref, nodes_ref, mids_ref,
    w_ei, w_eo, w_ni, w_no, w_up, w_mi, w_mo, w_di,
    fine_ref, mid_ref,
    hid_v, proj_v, nodes_v, halo, mids_v, v_ei, v_eo, v_ni, v_no, v_up, v_mi, v_mo, v_di,
    acc, hot_s, hot_r, up_s, up_r, dn_s, dn_r,
    load_sem, halo_send, halo_recv, send_sem, recv_sem,
):
    n, d = nodes_v.shape
    m = mids_v.shape[0]
    pairs = n_dev // 2
    slots = n_dev * 12
    grp, dev = lax.axis_index("grp"), lax.axis_index("dev")
    lin = grp * n_dev + dev
    total = n_grp * n_dev
    nxt, prv = lax.rem(lin + 1, total), lax.rem(lin + total - 1, total)
    next_id = (nxt // n_dev, lax.rem(nxt, n_dev))
    prev_id = (prv // n_dev, lax.rem(prv, n_dev))

    loads = []
    for j, (src, dst) in enumerate((
        (nodes_ref, nodes_v), (w_ei, v_ei), (w_ni, v_ni), (w_eo, v_eo), (w_no, v_no), (w_up, v_up),
        (mids_ref, mids_v), (w_mi, v_mi), (w_mo, v_mo), (w_di, v_di),
    )):
        copy = pltpu.make_async_copy(src, dst, load_sem.at[j])
        copy.start()
        loads.append(copy)
    l_nodes, l_ei, l_ni, l_eo, l_no, l_up, l_mids, l_mi, l_mo, l_di = loads

    barrier = pltpu.get_barrier_semaphore()

    @pl.loop(1, n_dev)
    def _(k):
        pl.semaphore_signal(barrier, inc=1, device_id=(grp, lax.rem(dev + k, n_dev)), device_id_type=MESH)

    pl.semaphore_signal(barrier, inc=1, device_id=next_id, device_id_type=MESH)
    pl.semaphore_signal(barrier, inc=1, device_id=prev_id, device_id_type=MESH)
    pl.semaphore_wait(barrier, n_dev + 1)

    to_next = pltpu.make_async_remote_copy(
        src_ref=nodes_ref, dst_ref=halo.at[0], send_sem=halo_send.at[0], recv_sem=halo_recv.at[0],
        device_id=next_id, device_id_type=MESH)
    to_prev = pltpu.make_async_remote_copy(
        src_ref=nodes_ref, dst_ref=halo.at[1], send_sem=halo_send.at[1], recv_sem=halo_recv.at[1],
        device_id=prev_id, device_id_type=MESH)
    to_next.start()
    to_prev.start()

    def send_all(src, dst, j):
        @pl.loop(1, n_dev)
        def _(k):
            peer = lax.rem(dev + k, n_dev)
            pltpu.make_async_remote_copy(
                src_ref=src.at[peer], dst_ref=dst.at[dev], send_sem=send_sem.at[j], recv_sem=recv_sem.at[j],
                device_id=(grp, peer), device_id_type=MESH).start()

        dst[dev] = src[dev]

    def wait_all(buf, sem):
        part = buf.at[pl.ds(0, n_dev - 1)]
        pltpu.make_async_copy(part, part, sem).wait()

    ints = ints_ref[...]
    by_row = ints.astype(F32).T
    owner_row = by_row[6:7, :]
    owner_hot = hot(lax.broadcasted_iota(jnp.int32, (n_dev, n), 0).astype(F32) == owner_row)
    earlier = hot(lax.broadcasted_iota(jnp.int32, (n, n), 0) < lax.broadcasted_iota(jnp.int32, (n, n), 1))
    before = mm(owner_hot, earlier)
    rank = jnp.sum(before * owner_hot.astype(F32), axis=0, keepdims=True).astype(jnp.int32)
    owner_i = owner_row.astype(jnp.int32)
    place = ((owner_i >> 1) * 3 + (rank >> 2)) * 8 + (owner_i & 1) * 4 + (rank & 3)
    placing_t = hot(lax.broadcasted_iota(jnp.int32, (slots, n), 0) == place)
    slot_hot = hot(lax.broadcasted_iota(jnp.int32, (n, 128), 1) == ints[:, 7:8])
    hot_s[...] = pack_hot(mm(placing_t, slot_hot), pairs)
    send_all(hot_s, hot_r, 0)

    l_nodes.wait()
    l_ei.wait()
    own = nodes_v[...]
    proj_v[0:n, :] = mm(own, v_ei[0:d, :]).astype(BF)
    dst_proj = mm(own, v_ei[d : 2 * d, :])
    lanes = lax.broadcasted_iota(jnp.int32, (n, n), 1)
    for k in range(6):
        acc[k] = dst_proj + mm(hot(lanes + n == ints[:, k : k + 1]), proj_v[0:n, :])
    l_ni.wait()
    node_top = mm(own, v_ni[0:d, :])

    to_next.wait()
    to_prev.wait()
    around = halo[...].reshape(2 * n, d)
    proj_v[n : 3 * n, :] = mm(around, v_ei[0:d, :]).astype(BF)
    part = n // 3

    @pl.loop(0, 3)
    def _(j):
        rows = pl.ds(pl.multiple_of(j * part, part), part)
        lanes = lax.broadcasted_iota(jnp.int32, (part, 2 * n), 1)
        lanes = jnp.where(lanes < n, lanes, lanes + n)
        mine = ints_ref[rows, :]
        hidden = jnp.zeros((part, d), F32)
        for k in range(6):
            hidden = hidden + silu(acc[k, rows, :] + mm(hot(lanes == mine[:, k : k + 1]), proj_v[n : 3 * n, :]))
        hid_v[rows, :] = hidden.astype(BF)

    l_eo.wait()
    agg = mm(hid_v[...], v_eo[...]).astype(BF)
    node_hidden = silu(node_top + mm(agg, v_ni[d : 2 * d, :])).astype(BF)
    l_no.wait()
    fine_new = (own.astype(F32) + mm(node_hidden, v_no[...])).astype(BF)
    l_up.wait()
    up_msg = silu(mm(fine_new, v_up[...])).astype(BF)
    up_s[...] = pack(mm(placing_t, up_msg), pairs)
    send_all(up_s, up_r, 1)

    l_di.wait()
    acc[0] = mm(fine_new, v_di[0:d, :])
    acc[1] = fine_new.astype(F32)
    l_mids.wait()
    l_mi.wait()
    mids = mids_v[...]
    mid_top = mm(mids, v_mi[0:d, :])
    l_mo.wait()
    wait_all(hot_r, recv_sem.at[0])
    wait_all(hot_s, send_sem.at[0])
    got_hot = unpack_hot(hot_r[...], pairs)
    got_hot_t = got_hot.T.astype(BF)[0:m, :]
    got_hot = got_hot.astype(BF)[:, 0:m]
    place_b = jnp.broadcast_to(place.astype(F32), (128, n)).T
    placing = jnp.concatenate(
        [hot(place_b == (lax.broadcasted_iota(jnp.int32, (n, 128), 1) + 128 * j).astype(F32)) for j in range(slots // 128)],
        axis=1)

    wait_all(up_r, recv_sem.at[1])
    up_sum = mm(got_hot_t, unpack(up_r[...], pairs)).astype(BF)
    mid_hidden = silu(mid_top + mm(up_sum, v_mi[d : 2 * d, :])).astype(BF)
    mid_new = (mids.astype(F32) + mm(mid_hidden, v_mo[...])).astype(BF)
    dn_s[...] = pack(mm(got_hot, mid_new), pairs)
    send_all(dn_s, dn_r, 2)
    mid_ref[...] = mid_new
    wait_all(up_s, send_sem.at[1])

    wait_all(dn_r, recv_sem.at[2])
    parents = mm(placing, unpack(dn_r[...], pairs)).astype(BF)
    down = silu(acc[0] + mm(parents, v_di[d : 2 * d, :]))
    fine_ref[...] = (acc[1] + down).astype(BF)
    wait_all(dn_s, send_sem.at[2])


def body(n_grp, n_dev, nodes, senders, mid_nodes, owners, slots, *weights):
    n, d = nodes.shape
    m = mid_nodes.shape[0]
    ints = jnp.concatenate([senders.reshape(n, 6), owners, slots[:, None]], axis=1)
    ints = jnp.pad(ints, ((0, 0), (0, 120)))
    vmem = pl.BlockSpec(memory_space=pltpu.VMEM)
    any_ = pl.BlockSpec(memory_space=pl.ANY)
    block = pltpu.VMEM((n_dev, 3, 16, 128), BF)
    hot_block = pltpu.VMEM((n_dev, 16, 128), BF)
    return pl.pallas_call(
        functools.partial(kernel, n_grp, n_dev),
        out_shape=(jax.ShapeDtypeStruct((n, d), BF), jax.ShapeDtypeStruct((m, d), BF)),
        in_specs=[vmem] + [any_] * (2 + len(weights)),
        out_specs=(vmem, vmem),
        scratch_shapes=[pltpu.VMEM((n, d), BF), pltpu.VMEM((3 * n, d), BF), pltpu.VMEM((n, d), BF), pltpu.VMEM((2, n, d), BF), pltpu.VMEM((m, d), BF)]
        + [pltpu.VMEM(w.shape, BF) for w in weights]
        + [pltpu.VMEM((6, n, d), F32), hot_block, hot_block, block, block, block, block]
        + [
            pltpu.SemaphoreType.DMA((10,)),
            pltpu.SemaphoreType.DMA((2,)),
            pltpu.SemaphoreType.DMA((2,)),
            pltpu.SemaphoreType.DMA((3,)),
            pltpu.SemaphoreType.DMA((3,)),
        ],
        compiler_params=pltpu.CompilerParams(
            collective_id=0, has_side_effects=True, vmem_limit_bytes=48 * 1024 * 1024),
        cost_estimate=pl.CostEstimate(flops=7_000_000_000, bytes_accessed=10_000_000, transcendentals=2_000_000),
        name="sweep",
    )(ints, nodes, mid_nodes, *weights)


def solution(mesh):
    sharded, rows, copied = P(BOTH, None), P(BOTH), P()
    return jax.shard_map(
        functools.partial(body, mesh.shape["grp"], mesh.shape["dev"]),
        mesh=mesh,
        in_specs=(sharded, rows, sharded, sharded, rows) + (copied,) * 8,
        out_specs=(sharded, sharded),
        check_vma=False,
    )
```

time: 135 us -> 82.2 us (0.61)
  the two profiles are of different devices: /device:TPU:38 before, /device:TPU:1 now
where the time goes in v1:
time: 82.2 us; the launch traced here: 81.8 us
  Pallas kernels  70.7 us (86%)
  local copies, waits for them, and re-layouts  10.2 us (12%)
    pallas_call x1, Pallas kernels, body(): pl.pallas_call(functools.partial(kernel, n_grp, n_dev), out_shape=(jax.Sh...  70.7 us
    unnamed x19, local copies, waits for them, and re-layouts  8.44 us

profile of v1, /device:TPU:1, one launch (start us, length us, event | category | flops | bytes accessed | tf_op | source)
XLA Modules:
  0.0 81.8 jit_solution(16973841187296483408)
XLA Ops:
  0.6 0.0 copy-start
  0.6 1.0 %reshape.7 = s32[384,6]{1,0:T(8,128)S(1)} reshape(s32[2304]{0:T(1024)} %param.14) | data formatting | bytes 18432 | tf_op jit(solution)/shard_map/reshape | solution.py:229
  1.6 0.8 copy.20
  2.4 0.8 broadcast_in_dim.4
  3.2 0.0 copy-start.2
  3.2 0.2 pad_add_fusion
  3.4 0.0 copy-start.7
  3.5 0.0 copy-done
  3.5 0.8 copy-done.2
  4.3 0.1 copy-done.7
  4.4 0.0 copy-start.1
  4.4 1.2 %copy-done.1 = bf16[1024,512]{1,0:T(8,128)(2,1)S(1)} copy-done((bf16[1024,512]{1,0:T(8,128)(2,1)S(1)}, bf16[1024,512]{1,0:T(8,128)(2,1)}, u32[]{:S(2)}) %copy-start.1) | copy-done | bytes 1048600
  5.6 0.0 copy-start.3
  5.6 1.0 %copy-done.3 = bf16[512,512]{1,0:T(8,128)(2,1)S(1)} copy-done((bf16[512,512]{1,0:T(8,128)(2,1)S(1)}, bf16[512,512]{1,0:T(8,128)(2,1)}, u32[]{:S(2)}) %copy-start.3) | copy-done | bytes 524312
  6.6 0.0 copy-start.4
  6.6 1.0 %copy-done.4 = bf16[512,512]{1,0:T(8,128)(2,1)S(1)} copy-done((bf16[512,512]{1,0:T(8,128)(2,1)S(1)}, bf16[512,512]{1,0:T(8,128)(2,1)}, u32[]{:S(2)}) %copy-start.4) | copy-done | bytes 524312
  7.7 0.0 copy-start.5
  7.7 1.0 %copy-done.5 = bf16[512,512]{1,0:T(8,128)(2,1)S(1)} copy-done((bf16[512,512]{1,0:T(8,128)(2,1)S(1)}, bf16[512,512]{1,0:T(8,128)(2,1)}, u32[]{:S(2)}) %copy-start.5) | copy-done | bytes 524312
  8.7 0.0 copy-start.6
  8.7 1.0 %copy-done.6 = bf16[384,512]{1,0:T(8,128)(2,1)S(1)} copy-done((bf16[384,512]{1,0:T(8,128)(2,1)S(1)}, bf16[384,512]{1,0:T(8,128)(2,1)}, u32[]{:S(2)}) %copy-start.6) | copy-done | bytes 393240
  9.7 70.7 %sweep.1 = (bf16[384,512]{1,0:T(8,128)(2,1)S(1)}, bf16[96,512]{1,0:T(8,128)(2,1)S(1)}) custom-call(s32[384,128]{1,0:T(8,128)S(1)} %pad.4.ints_ref, bf16[384,512]{1,0:T(8,128)(2,1)S(1)} %copy-done.6, bf16[96,512]{1,0:T(8,128)(2,1)S(1)} %copy-done.7, bf16[1024,512]{1,0:T(8,128)(2,1)S(1)} %copy-done, bf16[512,512]{1,0:T(8,128)(2,1)S(1)} %copy-done.2, ...), custom_call_target="tpu_custom_call" | custom-call | flops 7000000000 | bytes 10000000 | tf_op jit(solution)/shard_map/sweep/pallas_call | solution.py:235
  80.4 0.7 copy.24
  81.2 0.6 copy.25
  (1 shorter events, 0.0 us)
Async XLA Ops:
  0.6 2.8 %copy-start = (bf16[1024,512]{1,0:T(8,128)(2,1)S(1)}, bf16[1024,512]{1,0:T(8,128)(2,1)}, u32[]{:S(2)}) copy-start(bf16[1024,512]{1,0:T(8,128)(2,1)} %w_ei.1) | copy-start | bytes 3145732
  3.2 1.0 %copy-start.2 = (bf16[512,512]{1,0:T(8,128)(2,1)S(1)}, bf16[512,512]{1,0:T(8,128)(2,1)}, u32[]{:S(2)}) copy-start(bf16[512,512]{1,0:T(8,128)(2,1)} %w_eo.1) | copy-start | bytes 1572868
  3.4 0.9 %copy-start.7 = (bf16[96,512]{1,0:T(8,128)(2,1)S(1)}, bf16[96,512]{1,0:T(8,128)(2,1)}, u32[]{:S(2)}) copy-start(bf16[96,512]{1,0:T(8,128)(2,1)} %mids_ref.1) | copy-start | bytes 294916
  4.4 1.2 %copy-start.1 = (bf16[1024,512]{1,0:T(8,128)(2,1)S(1)}, bf16[1024,512]{1,0:T(8,128)(2,1)}, u32[]{:S(2)}) copy-start(bf16[1024,512]{1,0:T(8,128)(2,1)} %w_ni.1) | copy-start | bytes 3145732
  5.6 1.0 %copy-start.3 = (bf16[512,512]{1,0:T(8,128)(2,1)S(1)}, bf16[512,512]{1,0:T(8,128)(2,1)}, u32[]{:S(2)}) copy-start(bf16[512,512]{1,0:T(8,128)(2,1)} %w_no.1) | copy-start | bytes 1572868
  6.6 1.0 %copy-start.4 = (bf16[512,512]{1,0:T(8,128)(2,1)S(1)}, bf16[512,512]{1,0:T(8,128)(2,1)}, u32[]{:S(2)}) copy-start(bf16[512,512]{1,0:T(8,128)(2,1)} %w_up.1) | copy-start | bytes 1572868
  7.7 1.0 %copy-start.5 = (bf16[512,512]{1,0:T(8,128)(2,1)S(1)}, bf16[512,512]{1,0:T(8,128)(2,1)}, u32[]{:S(2)}) copy-start(bf16[512,512]{1,0:T(8,128)(2,1)} %w_mo.1) | copy-start | bytes 1572868
  8.7 1.0 %copy-start.6 = (bf16[384,512]{1,0:T(8,128)(2,1)S(1)}, bf16[384,512]{1,0:T(8,128)(2,1)}, u32[]{:S(2)}) copy-start(bf16[384,512]{1,0:T(8,128)(2,1)} %nodes_ref.1) | copy-start | bytes 1179652

commit v2 on v1

v2 whole, which is shorter than its diff:
```python
import functools

import jax
import jax.numpy as jnp
from jax import lax
from jax.experimental import pallas as pl
from jax.experimental.pallas import tpu as pltpu
from jax.sharding import PartitionSpec as P

MESH = pl.DeviceIdType.MESH
BOTH = ("grp", "dev")
BF = jnp.bfloat16
F32 = jnp.float32


def silu(x):
    half = 0.5 * x
    return half + half * jnp.tanh(half)


def mm(a, b):
    return jnp.dot(a, b, preferred_element_type=F32)


def hot(match):
    return jnp.where(match, 1.0, 0.0).astype(BF)


N_Z, N_Q = 8, 8
ORDER = (0, 7, 1, 6, 2, 5, 3, 4)


def kernel(
    n_grp, n_dev,
    edges_ref, owner_ref, slot_ref, nodes_ref, mids_ref,
    w_ei, w_eo, w_ni, w_no, w_up, w_mi, w_mo, w_di,
    fine_ref, mid_ref,
    parents_v, got_v, got_t, from_v, hid_v, proj_v, nodes_v, halo, mids_v, v_ei, v_eo, v_ni, v_no, v_up, v_mi, v_mo, v_di,
    acc, code_s, code_r, up_s, up_r, dn_s, dn_r, sums, ring_s, ring_r, ag,
    load_sem, halo_send, halo_recv, code_send, code_recv, up_send, up_recv, dn_send, dn_recv,
    rs_send, rs_recv, ag_send, ag_recv,
):
    n, d = nodes_v.shape
    m = mids_v.shape[0]
    grp, dev = lax.axis_index("grp"), lax.axis_index("dev")
    lin = grp * n_dev + dev
    total = n_grp * n_dev
    nxt, prv = lax.rem(lin + 1, total), lax.rem(lin + total - 1, total)
    next_id = (nxt // n_dev, lax.rem(nxt, n_dev))
    prev_id = (prv // n_dev, lax.rem(prv, n_dev))

    loads = []
    for j, (src, dst) in enumerate((
        (nodes_ref, nodes_v), (w_ei, v_ei), (w_ni, v_ni), (w_eo, v_eo), (w_no, v_no), (w_up, v_up),
        (mids_ref, mids_v), (w_mi, v_mi), (w_mo, v_mo), (w_di, v_di),
    )):
        copy = pltpu.make_async_copy(src, dst, load_sem.at[j])
        copy.start()
        loads.append(copy)
    l_nodes, l_ei, l_ni, l_eo, l_no, l_up, l_mids, l_mi, l_mo, l_di = loads

    barrier = pltpu.get_barrier_semaphore()

    core, line = lax.rem(dev, 2), lax.div(dev, 2)
    z, y = lax.rem(line, N_Z), lax.div(line, N_Z)
    q = y * 2 + core

    def at(q_to, z_to):
        return (grp, (lax.div(q_to, 2) * N_Z + z_to) * 2 + lax.rem(q_to, 2))

    ring_id = (at(q, lax.rem(z + 1, N_Z)), at(q, lax.rem(z + N_Z - 1, N_Z)))
    peers = [lax.rem(q + k, N_Q) for k in range(1, N_Q)]
    for other in [at(p, z) for p in peers] + list(ring_id):
        pl.semaphore_signal(barrier, inc=1, device_id=other, device_id_type=MESH)
    pl.semaphore_signal(barrier, inc=1, device_id=next_id, device_id_type=MESH)
    pl.semaphore_signal(barrier, inc=1, device_id=prev_id, device_id_type=MESH)
    pl.semaphore_wait(barrier, N_Q + 3)

    to_next = pltpu.make_async_remote_copy(
        src_ref=nodes_ref, dst_ref=halo.at[0], send_sem=halo_send.at[0], recv_sem=halo_recv.at[0],
        device_id=next_id, device_id_type=MESH)
    to_prev = pltpu.make_async_remote_copy(
        src_ref=nodes_ref, dst_ref=halo.at[1], send_sem=halo_send.at[1], recv_sem=halo_recv.at[1],
        device_id=prev_id, device_id_type=MESH)
    to_next.start()
    to_prev.start()

    def send_all(src, dst, send, recv):
        for p in peers:
            pltpu.make_async_remote_copy(
                src_ref=src.at[p], dst_ref=dst.at[q], send_sem=send, recv_sem=recv,
                device_id=at(p, z), device_id_type=MESH).start()
        dst[q] = src[q]

    def wait_all(buf, sem):
        some = buf.at[pl.ds(0, N_Q - 1)]
        pltpu.make_async_copy(some, some, sem).wait()

    def ring(src, dst, send, recv, way, step, half):
        rows = pl.ds(half * (m // 2), m // 2)
        return pltpu.make_async_remote_copy(
            src_ref=src.at[rows], dst_ref=dst.at[rows],
            send_sem=send.at[way * 4 + step, half], recv_sem=recv.at[way * 4 + step, half],
            device_id=ring_id[way], device_id_type=MESH)

    owner = owner_ref[...]
    ahead = (((owner >> 1) & 7) - z) & 7
    turn = jnp.where(ahead < 4, 2 * ahead, 15 - 2 * ahead)
    owner_q = (owner >> 4) * 2 + (owner & 1)
    block_ids = lax.broadcasted_iota(jnp.int32, (n_dev, n), 0)
    owner_hot = hot(block_ids == turn * 8 + owner_q)
    earlier = hot(lax.broadcasted_iota(jnp.int32, (n, n), 0) < lax.broadcasted_iota(jnp.int32, (n, n), 1))
    before = mm(owner_hot, earlier)
    rank = jnp.sum(before * owner_hot.astype(F32), axis=0, keepdims=True).astype(jnp.int32)
    place = (turn * 8 + owner_q) * 16 + rank
    ranked = jnp.where(lax.broadcasted_iota(jnp.int32, (128, n), 0) == rank, slot_ref[...] + 1, 0)
    ranked = ranked.astype(F32).astype(BF)
    code = lax.dot_general(
        hot(block_ids == owner_q * 8 + turn), ranked, (((1,), (1,)), ((), ())), preferred_element_type=F32)
    code_s[...] = code.reshape(N_Q, 8, 128)
    send_all(code_s, code_r, code_send.at[0], code_recv.at[0])

    flat = edges_ref[...]
    parts = jnp.concatenate([flat >> 5, flat & 31], axis=1).astype(F32).astype(BF)
    lines = flat.shape[0]
    row_ids = lax.broadcasted_iota(jnp.int32, (n, 32), 0)
    line_ids = lax.broadcasted_iota(jnp.int32, (n, 32), 1)
    lane_ids = lax.broadcasted_iota(jnp.int32, (n, 128), 1)
    edge_ids = lax.broadcasted_iota(jnp.int32, (n, 128), 0) * 6
    parts = jnp.concatenate([parts, jnp.zeros((32 - lines, 256), BF)], axis=0)
    for k in range(6):
        line = mm(hot(line_ids == (row_ids * 6 + k) >> 7), parts)
        line = line[:, 0:128] * 32.0 + line[:, 128:256]
        line = jnp.where(lane_ids == ((edge_ids + k) & 127), line, 0.0)
        from_v[:, k : k + 1] = jnp.sum(line, axis=1, keepdims=True).astype(jnp.int32)

    l_nodes.wait()
    l_ei.wait()
    own = nodes_v[...]
    proj_v[0:n, :] = mm(own, v_ei[0:d, :]).astype(BF)
    dst_proj = mm(own, v_ei[d : 2 * d, :])
    ints = from_v[...]
    lanes = lax.broadcasted_iota(jnp.int32, (n, n), 1)
    for k in range(6):
        acc[k] = dst_proj + mm(hot(lanes + n == ints[:, k : k + 1]), proj_v[0:n, :])
    l_ni.wait()
    node_top = mm(own, v_ni[0:d, :])

    wait_all(code_r, code_recv.at[0])
    wait_all(code_s, code_send.at[0])
    got = code_r[...].reshape(n_dev, 128).astype(BF)
    rows = lax.broadcasted_iota(jnp.int32, (16 * n_dev, n_dev), 0)
    line = mm(hot(lax.broadcasted_iota(jnp.int32, (16 * n_dev, n_dev), 1) == ((rows >> 4) & 7) * 8 + (rows >> 7)), got)
    rows = lax.broadcasted_iota(jnp.int32, (16 * n_dev, 128), 0)
    cols = lax.broadcasted_iota(jnp.int32, (16 * n_dev, 128), 1)
    line = jnp.where(cols == (rows & 15), line, 0.0)
    line = jnp.sum(line, axis=1, keepdims=True).astype(jnp.int32) - 1
    got_hot = jnp.where(cols == line, 1.0, 0.0)
    for j in range(8):
        got_t[j] = got_hot[128 * j : 128 * (j + 1)].T.astype(BF)
    got_v[...] = got_hot.astype(BF)

    to_next.wait()
    to_prev.wait()
    around = halo[...].reshape(2 * n, d)
    proj_v[n : 3 * n, :] = mm(around, v_ei[0:d, :]).astype(BF)
    part = n // 3

    @pl.loop(0, 3)
    def _(j):
        rows = pl.ds(pl.multiple_of(j * part, part), part)
        lanes = lax.broadcasted_iota(jnp.int32, (part, 2 * n), 1)
        lanes = jnp.where(lanes < n, lanes, lanes + n)
        mine = from_v[rows, :]
        hidden = jnp.zeros((part, d), F32)
        for k in range(6):
            hidden = hidden + silu(acc[k, rows, :] + mm(hot(lanes == mine[:, k : k + 1]), proj_v[n : 3 * n, :]))
        hid_v[rows, :] = hidden.astype(BF)

    l_eo.wait()
    agg = mm(hid_v[...], v_eo[...]).astype(BF)
    node_hidden = silu(node_top + mm(agg, v_ni[d : 2 * d, :])).astype(BF)
    l_no.wait()
    fine_new = (own.astype(F32) + mm(node_hidden, v_no[...])).astype(BF)
    l_up.wait()
    up_msg = silu(mm(fine_new, v_up[...])).astype(BF)
    slot_ids = lax.broadcasted_iota(jnp.int32, (128, n), 0)
    for j in range(7, -1, -1):
        up_s[j] = mm(hot(slot_ids + 128 * j == place), up_msg).astype(BF).reshape(N_Q, 16, d)
        send_all(up_s.at[j], up_r.at[j], up_send.at[j], up_recv.at[j])

    l_di.wait()
    acc[0] = mm(fine_new, v_di[0:d, :])
    acc[1] = fine_new.astype(F32)
    l_mids.wait()
    l_mi.wait()
    mids = mids_v[...]
    mid_top = mm(mids, v_mi[0:d, :])
    l_mo.wait()
    place_b = jnp.broadcast_to(place.astype(F32), (128, n)).T
    placing = jnp.concatenate(
        [hot(place_b == (lax.broadcasted_iota(jnp.int32, (n, 128), 1) + 128 * j).astype(F32)) for j in range(8)],
        axis=1)

    def gather(j):
        wait_all(up_r.at[j], up_recv.at[j])
        sums[ORDER[j]] = mm(got_t[j][0:m, :], up_r[j].reshape(128, d))

    def pass_on(way, step):
        ahead = 4 - step if way == 0 else 5 + step
        slot = way * 4 + step
        for half in range(2):
            rows = slice(half * (m // 2), (half + 1) * (m // 2))
            value = sums[ahead, rows, :]
            if step > 0:
                ring(ring_s.at[slot - 1], ring_r.at[slot - 1], rs_send, rs_recv, way, step - 1, half).wait_recv()
                value = value + ring_r[slot - 1, rows, :].astype(F32)
            ring_s[slot, rows, :] = value.astype(BF)
            ring(ring_s.at[slot], ring_r.at[slot], rs_send, rs_recv, way, step, half).start()

    gather(7)
    pass_on(0, 0)
    gather(6)
    gather(5)
    pass_on(1, 0)
    pass_on(0, 1)
    gather(4)
    gather(3)
    pass_on(1, 1)
    pass_on(0, 2)
    gather(2)
    gather(1)
    pass_on(1, 2)
    pass_on(0, 3)
    gather(0)
    for half in range(2):
        ring(ring_s.at[6], ring_r.at[6], rs_send, rs_recv, 1, 2, half).wait_recv()
    for half in range(2):
        ring(ring_s.at[3], ring_r.at[3], rs_send, rs_recv, 0, 3, half).wait_recv()
    up_sum = (sums[0] + ring_r[6].astype(F32) + ring_r[3].astype(F32)).astype(BF)
    mid_hidden = silu(mid_top + mm(up_sum, v_mi[d : 2 * d, :])).astype(BF)
    mid_new = (mids.astype(F32) + mm(mid_hidden, v_mo[...])).astype(BF)

    def step_of(way, step):
        return (step and 8 - step, 7 - step) if way == 0 else (step, step + 1)

    def hand_on(way, step, half):
        src, dst = step_of(way, step)
        return ring(ag.at[src], ag.at[dst], ag_send, ag_recv, way, step, half)

    def pick(j):
        picked = mm(got_v[128 * j : 128 * (j + 1), 0:m], ag[ORDER[j]])
        dn_s[j] = picked.astype(BF).reshape(N_Q, 16, d)
        send_all(dn_s.at[j], dn_r.at[j], dn_send.at[j], dn_recv.at[j])

    ag[0] = mid_new
    for half in range(2):
        for way in range(2):
            hand_on(way, 0, half).start()
    pick(0)
    mid_ref[...] = mid_new
    for step in range(4):
        ways = (0, 1) if step < 3 else (0,)
        for half in range(2):
            for way in ways:
                hand_on(way, step, half).wait_recv()
                if step + 1 < (4, 3)[way]:
                    hand_on(way, step + 1, half).start()
        for way in ways:
            pick(2 * step + 1 + way)

    for j in range(4):
        wait_all(dn_r.at[j], dn_recv.at[j])
    parents_v[...] = mm(placing[:, 0:512], dn_r[0:4].reshape(512, d))
    for j in range(4, 8):
        wait_all(dn_r.at[j], dn_recv.at[j])
    parents = (parents_v[...] + mm(placing[:, 512:1024], dn_r[4:8].reshape(512, d))).astype(BF)
    down = silu(acc[0] + mm(parents, v_di[d : 2 * d, :]))
    fine_ref[...] = (acc[1] + down).astype(BF)
    for j in range(8):
        wait_all(up_s.at[j], up_send.at[j])
        wait_all(dn_s.at[j], dn_send.at[j])
    for way in range(2):
        for step in range((4, 3)[way]):
            for half in range(2):
                ring(ring_s.at[way * 4 + step], ring_r.at[way * 4 + step], rs_send, rs_recv, way, step, half).wait_send()
                hand_on(way, step, half).wait_send()


def body(n_grp, n_dev, nodes, senders, mid_nodes, owners, slots, *weights):
    n, d = nodes.shape
    m = mid_nodes.shape[0]
    vmem = pl.BlockSpec(memory_space=pltpu.VMEM)
    any_ = pl.BlockSpec(memory_space=pltpu.HBM)
    block = pltpu.VMEM((8, N_Q, 16, d), BF)
    code = pltpu.VMEM((N_Q, 8, 128), F32)
    return pl.pallas_call(
        functools.partial(kernel, n_grp, n_dev),
        out_shape=(jax.ShapeDtypeStruct((n, d), BF), jax.ShapeDtypeStruct((m, d), BF)),
        in_specs=[vmem] * 3 + [any_] * (2 + len(weights)),
        out_specs=(vmem, vmem),
        scratch_shapes=[pltpu.VMEM((n, d), F32), pltpu.VMEM((16 * n_dev, 128), BF), pltpu.VMEM((8, 128, 128), BF), pltpu.VMEM((n, 128), jnp.int32), pltpu.VMEM((n, d), BF), pltpu.VMEM((3 * n, d), BF), pltpu.VMEM((n, d), BF), pltpu.VMEM((2, n, d), BF), pltpu.VMEM((m, d), BF)]
        + [pltpu.VMEM(w.shape, BF) for w in weights]
        + [pltpu.VMEM((6, n, d), F32), code, code, block, block, block, block]
        + [pltpu.VMEM((8, m, d), F32), pltpu.VMEM((7, m, d), BF), pltpu.VMEM((7, m, d), BF), pltpu.VMEM((8, m, d), BF)]
        + [pltpu.SemaphoreType.DMA((k,)) for k in (10, 2, 2, 1, 1, 8, 8, 8, 8)]
        + [pltpu.SemaphoreType.DMA((7, 2))] * 4,
        compiler_params=pltpu.CompilerParams(
            collective_id=0, has_side_effects=True, vmem_limit_bytes=63 * 1024 * 1024),
        cost_estimate=pl.CostEstimate(flops=7_000_000_000, bytes_accessed=10_000_000, transcendentals=2_000_000),
        name="sweep",
    )(senders.reshape(-1, 128), owners.reshape(1, n), slots.reshape(1, n), nodes, mid_nodes, *weights)


def solution(mesh):
    sharded, rows, copied = P(BOTH, None), P(BOTH), P()
    return jax.shard_map(
        functools.partial(body, mesh.shape["grp"], mesh.shape["dev"]),
        mesh=mesh,
        in_specs=(sharded, rows, sharded, sharded, rows) + (copied,) * 8,
        out_specs=(sharded, sharded),
        check_vma=False,
    )
```

time: 82.2 us -> 70.2 us (0.85)
  local copies, waits for them, and re-layouts: 10.2 us -> 3.68 us
  Pallas kernels: 70.7 us -> 65.7 us
    unnamed x19 -> x6, local copies, waits for them, and re-layouts: 8.44 us -> 3.12 us
    pallas_call x1, Pallas kernels: 70.7 us -> 65.7 us  [body(): pl.pallas_call(functools.partial(kernel, n_grp, n_dev), out_shape=(jax.Sh...]
where the time goes in v2:
time: 70.2 us; the launch traced here: 70 us
  Pallas kernels  65.7 us (94%)
  local copies, waits for them, and re-layouts  3.68 us (5%)
    pallas_call x1, Pallas kernels, body(): pl.pallas_call(functools.partial(kernel, n_grp, n_dev), out_shape=(jax.Sh...  65.7 us
    unnamed x6, local copies, waits for them, and re-layouts  3.12 us

profile of v2, /device:TPU:1, one launch (start us, length us, event | category | flops | bytes accessed | tf_op | source)
XLA Modules:
  0.0 70.0 jit_solution(12288352494210858597)
XLA Ops:
  0.6 0.0 copy-start.1
  0.6 0.7 copy-done.1
  1.3 0.6 reshape.15.slot_ref
  1.9 65.7 %sweep.1 = (bf16[384,512]{1,0:T(8,128)(2,1)}, bf16[96,512]{1,0:T(8,128)(2,1)}) custom-call(s32[18,128]{1,0:T(8,128)} %bitcast.2, s32[1,384]{1,0:T(1,128)} %bitcast.3, s32[1,384]{1,0:T(1,128)} %reshape.15.slot_ref, bf16[384,512]{1,0:T(8,128)(2,1)} %nodes_ref.1, bf16[96,512]{1,0:T(8,128)(2,1)} %mids_ref.1, bf16[1024,512]{1,0:T(8,128)(2,1)} %w_ei.1, ...), custom_call_target="tpu_custom_call" | custom-call | flops 7000000000 | bytes 10000000 | tf_op jit(solution)/shard_map/sweep/pallas_call | solution.py:297
  67.6 0.0 copy-start
  67.6 1.8 %copy.17 = bf16[384,512]{1,0:T(8,128)(2,1)} copy(bf16[384,512]{1,0:T(8,128)(2,1)} %get-tuple-element.4) | data formatting | bytes 786432
  69.4 0.0 copy-done
  69.4 0.6 copy.18
Async XLA Ops:
  0.6 0.7 copy-start.1
  67.6 1.8 %copy-start = (bf16[96,512]{1,0:T(8,128)(2,1)S(1)}, bf16[96,512]{1,0:T(8,128)(2,1)}, u32[]{:S(2)}) copy-start(bf16[96,512]{1,0:T(8,128)(2,1)} %get-tuple-element.5) | copy-start | bytes 294916

commit v3 on v2

--- a/solution.py
+++ b/solution.py
@@ -26,8 +26,37 @@
     return jnp.where(match, 1.0, 0.0).astype(BF)
 
 
+def swap4(x):
+    return pltpu.roll(x, 4, 1)
+
+
+def pack(rows, pairs):
+    groups = rows.shape[0] // 8
+    t = [rows[:, 128 * j : 128 * (j + 1)].reshape(groups, 8, 128) for j in range(4)]
+    low = lax.broadcasted_iota(jnp.int32, (groups, 8, 128), 1) < 4
+    first = [jnp.where(low, t[j], swap4(t[j + 1])) for j in (0, 2)]
+    second = [jnp.where(low, swap4(t[j]), t[j + 1]) for j in (0, 2)]
+    first = jnp.concatenate(first, axis=1).astype(BF).reshape(pairs, 1, 3, 16, 128)
+    second = jnp.concatenate(second, axis=1).astype(BF).reshape(pairs, 1, 3, 16, 128)
+    return jnp.concatenate([first, second], axis=1).reshape(2 * pairs, 3, 16, 128)
+
+
+def unpack(blocks, pairs):
+    both = blocks.astype(F32).reshape(pairs, 2, 3, 16, 128)
+    first = both[:, 0].reshape(pairs * 3, 16, 128)
+    second = both[:, 1].reshape(pairs * 3, 16, 128)
+    low = lax.broadcasted_iota(jnp.int32, (pairs * 3, 8, 128), 1) < 4
+    tiles = []
+    for piece in (slice(0, 8), slice(8, 16)):
+        a, b = first[:, piece], second[:, piece]
+        tiles.append(jnp.where(low, a, swap4(b)).reshape(pairs * 24, 128).astype(BF))
+        tiles.append(jnp.where(low, swap4(a), b).reshape(pairs * 24, 128).astype(BF))
+    return jnp.concatenate(tiles, axis=1)
+
+
 N_Z, N_Q = 8, 8
 ORDER = (0, 7, 1, 6, 2, 5, 3, 4)
+PIECES = 3
 
 
 def kernel(
@@ -96,11 +125,11 @@
         some = buf.at[pl.ds(0, N_Q - 1)]
         pltpu.make_async_copy(some, some, sem).wait()
 
-    def ring(src, dst, send, recv, way, step, half):
-        rows = pl.ds(half * (m // 2), m // 2)
+    def ring(src, dst, send, recv, way, step, piece):
+        rows = pl.ds(piece * (m // PIECES), m // PIECES)
         return pltpu.make_async_remote_copy(
             src_ref=src.at[rows], dst_ref=dst.at[rows],
-            send_sem=send.at[way * 4 + step, half], recv_sem=recv.at[way * 4 + step, half],
+            send_sem=send.at[way * 4 + step, piece], recv_sem=recv.at[way * 4 + step, piece],
             device_id=ring_id[way], device_id_type=MESH)
 
     owner = owner_ref[...]
@@ -112,8 +141,9 @@
     earlier = hot(lax.broadcasted_iota(jnp.int32, (n, n), 0) < lax.broadcasted_iota(jnp.int32, (n, n), 1))
     before = mm(owner_hot, earlier)
     rank = jnp.sum(before * owner_hot.astype(F32), axis=0, keepdims=True).astype(jnp.int32)
-    place = (turn * 8 + owner_q) * 16 + rank
-    ranked = jnp.where(lax.broadcasted_iota(jnp.int32, (128, n), 0) == rank, slot_ref[...] + 1, 0)
+    place = turn * 96 + ((owner_q >> 1) * 3 + (rank >> 2)) * 8 + (owner_q & 1) * 4 + (rank & 3)
+    slot_row = jnp.concatenate([slot_ref[j : j + 1, :] for j in range(n // 128)], axis=1)
+    ranked = jnp.where(lax.broadcasted_iota(jnp.int32, (128, n), 0) == rank, slot_row + 1, 0)
     ranked = ranked.astype(F32).astype(BF)
     code = lax.dot_general(
         hot(block_ids == owner_q * 8 + turn), ranked, (((1,), (1,)), ((), ())), preferred_element_type=F32)
@@ -150,10 +180,14 @@
     wait_all(code_s, code_send.at[0])
     got = code_r[...].reshape(n_dev, 128).astype(BF)
     rows = lax.broadcasted_iota(jnp.int32, (16 * n_dev, n_dev), 0)
-    line = mm(hot(lax.broadcasted_iota(jnp.int32, (16 * n_dev, n_dev), 1) == ((rows >> 4) & 7) * 8 + (rows >> 7)), got)
+    triple = (((rows & 127) >> 3) * 43691) >> 17
+    source = (2 * triple + ((rows >> 2) & 1)) * 8 + (rows >> 7)
+    line = mm(hot((lax.broadcasted_iota(jnp.int32, (16 * n_dev, n_dev), 1) == source) & ((rows & 127) < 96)), got)
     rows = lax.broadcasted_iota(jnp.int32, (16 * n_dev, 128), 0)
     cols = lax.broadcasted_iota(jnp.int32, (16 * n_dev, 128), 1)
-    line = jnp.where(cols == (rows & 15), line, 0.0)
+    group = (rows & 127) >> 3
+    rank_of = (group - 3 * ((group * 43691) >> 17)) * 4 + (rows & 3)
+    line = jnp.where(cols == rank_of, line, 0.0)
     line = jnp.sum(line, axis=1, keepdims=True).astype(jnp.int32) - 1
     got_hot = jnp.where(cols == line, 1.0, 0.0)
     for j in range(8):
@@ -184,9 +218,9 @@
     fine_new = (own.astype(F32) + mm(node_hidden, v_no[...])).astype(BF)
     l_up.wait()
     up_msg = silu(mm(fine_new, v_up[...])).astype(BF)
-    slot_ids = lax.broadcasted_iota(jnp.int32, (128, n), 0)
+    slot_ids = lax.broadcasted_iota(jnp.int32, (96, n), 0)
     for j in range(7, -1, -1):
-        up_s[j] = mm(hot(slot_ids + 128 * j == place), up_msg).astype(BF).reshape(N_Q, 16, d)
+        up_s[j] = pack(mm(hot(slot_ids + 96 * j == place), up_msg), N_Q // 2)
         send_all(up_s.at[j], up_r.at[j], up_send.at[j], up_recv.at[j])
 
     l_di.wait()
@@ -199,24 +233,24 @@
     l_mo.wait()
     place_b = jnp.broadcast_to(place.astype(F32), (128, n)).T
     placing = jnp.concatenate(
-        [hot(place_b == (lax.broadcasted_iota(jnp.int32, (n, 128), 1) + 128 * j).astype(F32)) for j in range(8)],
+        [hot(place_b == (lax.broadcasted_iota(jnp.int32, (n, 128), 1) + 128 * j).astype(F32)) for j in range(6)],
         axis=1)
 
     def gather(j):
         wait_all(up_r.at[j], up_recv.at[j])
-        sums[ORDER[j]] = mm(got_t[j][0:m, :], up_r[j].reshape(128, d))
+        sums[ORDER[j]] = mm(got_t[j][0:m, 0:96], unpack(up_r[j], N_Q // 2))
 
     def pass_on(way, step):
         ahead = 4 - step if way == 0 else 5 + step
         slot = way * 4 + step
-        for half in range(2):
-            rows = slice(half * (m // 2), (half + 1) * (m // 2))
+        for piece in range(PIECES):
+            rows = slice(piece * (m // PIECES), (piece + 1) * (m // PIECES))
             value = sums[ahead, rows, :]
             if step > 0:
-                ring(ring_s.at[slot - 1], ring_r.at[slot - 1], rs_send, rs_recv, way, step - 1, half).wait_recv()
+                ring(ring_s.at[slot - 1], ring_r.at[slot - 1], rs_send, rs_recv, way, step - 1, piece).wait_recv()
                 value = value + ring_r[slot - 1, rows, :].astype(F32)
             ring_s[slot, rows, :] = value.astype(BF)
-            ring(ring_s.at[slot], ring_r.at[slot], rs_send, rs_recv, way, step, half).start()
+            ring(ring_s.at[slot], ring_r.at[slot], rs_send, rs_recv, way, step, piece).start()
 
     gather(7)
     pass_on(0, 0)
@@ -233,10 +267,10 @@
     pass_on(1, 2)
     pass_on(0, 3)
     gather(0)
-    for half in range(2):
-        ring(ring_s.at[6], ring_r.at[6], rs_send, rs_recv, 1, 2, half).wait_recv()
-    for half in range(2):
-        ring(ring_s.at[3], ring_r.at[3], rs_send, rs_recv, 0, 3, half).wait_recv()
+    for piece in range(PIECES):
+        ring(ring_s.at[6], ring_r.at[6], rs_send, rs_recv, 1, 2, piece).wait_recv()
+    for piece in range(PIECES):
+        ring(ring_s.at[3], ring_r.at[3], rs_send, rs_recv, 0, 3, piece).wait_recv()
     up_sum = (sums[0] + ring_r[6].astype(F32) + ring_r[3].astype(F32)).astype(BF)
     mid_hidden = silu(mid_top + mm(up_sum, v_mi[d : 2 * d, :])).astype(BF)
     mid_new = (mids.astype(F32) + mm(mid_hidden, v_mo[...])).astype(BF)
@@ -244,37 +278,37 @@
     def step_of(way, step):
         return (step and 8 - step, 7 - step) if way == 0 else (step, step + 1)
 
-    def hand_on(way, step, half):
+    def hand_on(way, step, piece):
         src, dst = step_of(way, step)
-        return ring(ag.at[src], ag.at[dst], ag_send, ag_recv, way, step, half)
+        return ring(ag.at[src], ag.at[dst], ag_send, ag_recv, way, step, piece)
 
     def pick(j):
-        picked = mm(got_v[128 * j : 128 * (j + 1), 0:m], ag[ORDER[j]])
-        dn_s[j] = picked.astype(BF).reshape(N_Q, 16, d)
+        dn_s[j] = pack(mm(got_v[128 * j : 128 * j + 96, 0:m], ag[ORDER[j]]), N_Q // 2)
         send_all(dn_s.at[j], dn_r.at[j], dn_send.at[j], dn_recv.at[j])
 
     ag[0] = mid_new
-    for half in range(2):
+    for piece in range(PIECES):
         for way in range(2):
-            hand_on(way, 0, half).start()
+            hand_on(way, 0, piece).start()
     pick(0)
     mid_ref[...] = mid_new
     for step in range(4):
-        ways = (0, 1) if step < 3 else (0,)
-        for half in range(2):
-            for way in ways:
-                hand_on(way, step, half).wait_recv()
-                if step + 1 < (4, 3)[way]:
-                    hand_on(way, step + 1, half).start()
-        for way in ways:
+        for piece in range(PIECES):
+            for way in range(2):
+                if step < 3 or (piece == 2) == way:
+                    hand_on(way, step, piece).wait_recv()
+                if step < 2 or (step == 2 and (piece == 2) == way):
+                    hand_on(way, step + 1, piece).start()
+        for way in range(2 if step < 3 else 1):
             pick(2 * step + 1 + way)
 
-    for j in range(4):
-        wait_all(dn_r.at[j], dn_recv.at[j])
-    parents_v[...] = mm(placing[:, 0:512], dn_r[0:4].reshape(512, d))
-    for j in range(4, 8):
-        wait_all(dn_r.at[j], dn_recv.at[j])
-    parents = (parents_v[...] + mm(placing[:, 512:1024], dn_r[4:8].reshape(512, d))).astype(BF)
+    def landed(first, last):
+        for j in range(first, last):
+            wait_all(dn_r.at[j], dn_recv.at[j])
+        return jnp.concatenate([unpack(dn_r[j], N_Q // 2) for j in range(first, last)], axis=0)
+
+    parents_v[...] = mm(placing[:, 0:384], landed(0, 4))
+    parents = (parents_v[...] + mm(placing[:, 384:768], landed(4, 8))).astype(BF)
     down = silu(acc[0] + mm(parents, v_di[d : 2 * d, :]))
     fine_ref[...] = (acc[1] + down).astype(BF)
     for j in range(8):
@@ -282,9 +316,12 @@
         wait_all(dn_s.at[j], dn_send.at[j])
     for way in range(2):
         for step in range((4, 3)[way]):
-            for half in range(2):
-                ring(ring_s.at[way * 4 + step], ring_r.at[way * 4 + step], rs_send, rs_recv, way, step, half).wait_send()
-                hand_on(way, step, half).wait_send()
+            for piece in range(PIECES):
+                ring(ring_s.at[way * 4 + step], ring_r.at[way * 4 + step], rs_send, rs_recv, way, step, piece).wait_send()
+        for step in range(4):
+            for piece in range(PIECES):
+                if step < 3 or (piece == 2) == way:
+                    hand_on(way, step, piece).wait_send()
 
 
 def body(n_grp, n_dev, nodes, senders, mid_nodes, owners, slots, *weights):
@@ -292,7 +329,7 @@
     m = mid_nodes.shape[0]
     vmem = pl.BlockSpec(memory_space=pltpu.VMEM)
     any_ = pl.BlockSpec(memory_space=pltpu.HBM)
-    block = pltpu.VMEM((8, N_Q, 16, d), BF)
+    block = pltpu.VMEM((8, N_Q, 3, 16, 128), BF)
     code = pltpu.VMEM((N_Q, 8, 128), F32)
     return pl.pallas_call(
         functools.partial(kernel, n_grp, n_dev),
@@ -304,12 +341,12 @@
         + [pltpu.VMEM((6, n, d), F32), code, code, block, block, block, block]
         + [pltpu.VMEM((8, m, d), F32), pltpu.VMEM((7, m, d), BF), pltpu.VMEM((7, m, d), BF), pltpu.VMEM((8, m, d), BF)]
         + [pltpu.SemaphoreType.DMA((k,)) for k in (10, 2, 2, 1, 1, 8, 8, 8, 8)]
-        + [pltpu.SemaphoreType.DMA((7, 2))] * 4,
+        + [pltpu.SemaphoreType.DMA((8, PIECES))] * 4,
         compiler_params=pltpu.CompilerParams(
             collective_id=0, has_side_effects=True, vmem_limit_bytes=63 * 1024 * 1024),
         cost_estimate=pl.CostEstimate(flops=7_000_000_000, bytes_accessed=10_000_000, transcendentals=2_000_000),
         name="sweep",
-    )(senders.reshape(-1, 128), owners.reshape(1, n), slots.reshape(1, n), nodes, mid_nodes, *weights)
+    )(senders.reshape(-1, 128), owners.reshape(1, n), slots.reshape(n // 128, 128), nodes, mid_nodes, *weights)
 
 
 def solution(mesh):

time: 70.2 us -> 67.7 us (0.964)
  Pallas kernels: 65.7 us -> 64.4 us
  local copies, waits for them, and re-layouts: 3.68 us -> 2.45 us
    pallas_call x1, Pallas kernels: 65.7 us -> 64.4 us  [body(): pl.pallas_call(functools.partial(kernel, n_grp, n_dev), out_shape=(jax.Sh...]
    unnamed x6 -> x4, local copies, waits for them, and re-layouts: 3.12 us -> 2.45 us
where the time goes in v3:
time: 67.7 us; the launch traced here: 67.5 us
  Pallas kernels  64.4 us (95%)
  local copies, waits for them, and re-layouts  2.45 us (4%)
    pallas_call x1, Pallas kernels, body(): pl.pallas_call(functools.partial(kernel, n_grp, n_dev), out_shape=(jax.Sh...  64.4 us
    unnamed x4, local copies, waits for them, and re-layouts  2.45 us

profile of v3, /device:TPU:1, one launch (start us, length us, event | category | flops | bytes accessed | tf_op | source)
XLA Modules:
  0.0 67.5 jit_solution(12897363947492534523)
XLA Ops:
  0.6 64.4 %sweep.1 = (bf16[384,512]{1,0:T(8,128)(2,1)}, bf16[96,512]{1,0:T(8,128)(2,1)}) custom-call(s32[18,128]{1,0:T(8,128)} %bitcast.3, s32[1,384]{1,0:T(1,128)} %bitcast.5, s32[3,128]{1,0:T(4,128)} %bitcast.4, bf16[384,512]{1,0:T(8,128)(2,1)} %nodes_ref.1, bf16[96,512]{1,0:T(8,128)(2,1)} %mids_ref.1, bf16[1024,512]{1,0:T(8,128)(2,1)} %w_ei.1, ...), custom_call_target="tpu_custom_call" | custom-call | flops 7000000000 | bytes 10000000 | tf_op jit(solution)/shard_map/sweep/pallas_call | solution.py:334
  65.1 0.0 copy-start
  65.1 1.8 %copy.17 = bf16[384,512]{1,0:T(8,128)(2,1)} copy(bf16[384,512]{1,0:T(8,128)(2,1)} %get-tuple-element.4) | data formatting | bytes 786432
  66.9 0.0 copy-done
  66.9 0.6 copy.18
Async XLA Ops:
  65.1 1.8 %copy-start = (bf16[96,512]{1,0:T(8,128)(2,1)S(1)}, bf16[96,512]{1,0:T(8,128)(2,1)}, u32[]{:S(2)}) copy-start(bf16[96,512]{1,0:T(8,128)(2,1)} %get-tuple-element.5) | copy-start | bytes 294916

commit v4 on v3

--- a/solution.py
+++ b/solution.py
@@ -56,7 +56,7 @@
 
 N_Z, N_Q = 8, 8
 ORDER = (0, 7, 1, 6, 2, 5, 3, 4)
-PIECES = 3
+PIECES = 6
 
 
 def kernel(
@@ -194,21 +194,33 @@
         got_t[j] = got_hot[128 * j : 128 * (j + 1)].T.astype(BF)
     got_v[...] = got_hot.astype(BF)
 
-    to_next.wait()
-    to_prev.wait()
-    around = halo[...].reshape(2 * n, d)
-    proj_v[n : 3 * n, :] = mm(around, v_ei[0:d, :]).astype(BF)
+    early = 1 - core
     part = n // 3
+
+    def neighbour(side):
+        pltpu.make_async_copy(halo.at[side], halo.at[side], halo_recv.at[side]).wait()
+        proj_v[n : 2 * n, :] = mm(halo[side], v_ei[0:d, :]).astype(BF)
+
+    neighbour(early)
 
     @pl.loop(0, 3)
     def _(j):
         rows = pl.ds(pl.multiple_of(j * part, part), part)
-        lanes = lax.broadcasted_iota(jnp.int32, (part, 2 * n), 1)
-        lanes = jnp.where(lanes < n, lanes, lanes + n)
+        lanes = lax.broadcasted_iota(jnp.int32, (part, n), 1) + early * (2 * n)
+        mine = from_v[rows, :]
+        for k in range(6):
+            acc[k, rows, :] = acc[k, rows, :] + mm(hot(lanes == mine[:, k : k + 1]), proj_v[n : 2 * n, :])
+
+    neighbour(core)
+
+    @pl.loop(0, 3)
+    def _(j):
+        rows = pl.ds(pl.multiple_of(j * part, part), part)
+        lanes = lax.broadcasted_iota(jnp.int32, (part, n), 1) + core * (2 * n)
         mine = from_v[rows, :]
         hidden = jnp.zeros((part, d), F32)
         for k in range(6):
-            hidden = hidden + silu(acc[k, rows, :] + mm(hot(lanes == mine[:, k : k + 1]), proj_v[n : 3 * n, :]))
+            hidden = hidden + silu(acc[k, rows, :] + mm(hot(lanes == mine[:, k : k + 1]), proj_v[n : 2 * n, :]))
         hid_v[rows, :] = hidden.astype(BF)
 
     l_eo.wait()
@@ -295,9 +307,9 @@
     for step in range(4):
         for piece in range(PIECES):
             for way in range(2):
-                if step < 3 or (piece == 2) == way:
+                if step < 3 or (piece >= 3) == way:
                     hand_on(way, step, piece).wait_recv()
-                if step < 2 or (step == 2 and (piece == 2) == way):
+                if step < 2 or (step == 2 and (piece >= 3) == way):
                     hand_on(way, step + 1, piece).start()
         for way in range(2 if step < 3 else 1):
             pick(2 * step + 1 + way)
@@ -320,8 +332,10 @@
                 ring(ring_s.at[way * 4 + step], ring_r.at[way * 4 + step], rs_send, rs_recv, way, step, piece).wait_send()
         for step in range(4):
             for piece in range(PIECES):
-                if step < 3 or (piece == 2) == way:
+                if step < 3 or (piece >= 3) == way:
                     hand_on(way, step, piece).wait_send()
+    to_next.wait_send()
+    to_prev.wait_send()
 
 
 def body(n_grp, n_dev, nodes, senders, mid_nodes, owners, slots, *weights):
@@ -343,7 +357,7 @@
         + [pltpu.SemaphoreType.DMA((k,)) for k in (10, 2, 2, 1, 1, 8, 8, 8, 8)]
         + [pltpu.SemaphoreType.DMA((8, PIECES))] * 4,
         compiler_params=pltpu.CompilerParams(
-            collective_id=0, has_side_effects=True, vmem_limit_bytes=63 * 1024 * 1024),
+            collective_id=0, has_side_effects=True, vmem_limit_bytes=int(53.75 * 1024) * 1024),
         cost_estimate=pl.CostEstimate(flops=7_000_000_000, bytes_accessed=10_000_000, transcendentals=2_000_000),
         name="sweep",
     )(senders.reshape(-1, 128), owners.reshape(1, n), slots.reshape(n // 128, 128), nodes, mid_nodes, *weights)

time: 67.7 us -> 68 us (level)
  local copies, waits for them, and re-layouts: 2.45 us -> 3.79 us
  Pallas kernels: 64.4 us -> 63.4 us
    unnamed x4 -> x8, local copies, waits for them, and re-layouts: 2.45 us -> 3.79 us
    pallas_call x1, Pallas kernels: 64.4 us -> 63.4 us  [body(): pl.pallas_call(functools.partial(kernel, n_grp, n_dev), out_shape=(jax.Sh...]
where the time goes in v4:
time: 68 us; the launch traced here: 67.8 us
  Pallas kernels  63.4 us (93%)
  local copies, waits for them, and re-layouts  3.79 us (6%)
    pallas_call x1, Pallas kernels, body(): pl.pallas_call(functools.partial(kernel, n_grp, n_dev), out_shape=(jax.Sh...  63.4 us
    unnamed x8, local copies, waits for them, and re-layouts  3.79 us

profile of v4, /device:TPU:1, one launch (start us, length us, event | category | flops | bytes accessed | tf_op | source)
XLA Modules:
  0.0 67.8 jit_solution(2633042234050229400)
XLA Ops:
  0.6 0.0 copy-start.1
  0.6 0.0 copy-start.2
  0.7 0.7 copy-done.1
  1.3 0.0 copy-done.2
  1.3 0.0 copy-start
  1.3 0.7 %copy-done = s32[2304]{0:T(1024)S(1)} copy-done((s32[2304]{0:T(1024)S(1)}, s32[2304]{0:T(1024)}, u32[]{:S(2)}) %copy-start) | copy-done | bytes 9240
  2.0 63.4 %sweep.1 = (bf16[384,512]{1,0:T(8,128)(2,1)}, bf16[96,512]{1,0:T(8,128)(2,1)S(1)}) custom-call(s32[18,128]{1,0:T(8,128)S(1)} %bitcast.3, s32[1,384]{1,0:T(1,128)S(1)} %bitcast.5, s32[3,128]{1,0:T(4,128)S(1)} %bitcast.4, bf16[384,512]{1,0:T(8,128)(2,1)} %nodes_ref.1, bf16[96,512]{1,0:T(8,128)(2,1)} %mids_ref.1, bf16[1024,512]{1,0:T(8,128)(2,1)} %w_ei.1, ...), custom_call_target="tpu_custom_call" | custom-call | flops 7000000000 | bytes 10000000 | tf_op jit(solution)/shard_map/sweep/pallas_call | solution.py:348
  65.4 1.8 %copy.17 = bf16[384,512]{1,0:T(8,128)(2,1)} copy(bf16[384,512]{1,0:T(8,128)(2,1)} %get-tuple-element.4) | data formatting | bytes 786432
  67.2 0.6 copy.18
Async XLA Ops:
  0.6 0.7 %copy-start.1 = (s32[384]{0:T(512)S(1)}, s32[384]{0:T(512)}, u32[]{:S(2)}) copy-start(s32[384]{0:T(512)} %param.17) | copy-start | bytes 4612
  0.6 0.7 %copy-start.2 = (s32[384,1]{0,1:T(1,128)S(1)}, s32[384,1]{0,1:T(1,128)}, u32[]{:S(2)}) copy-start(s32[384,1]{0,1:T(1,128)} %param.16) | copy-start | bytes 4612
  1.3 0.7 %copy-start = (s32[2304]{0:T(1024)S(1)}, s32[2304]{0:T(1024)}, u32[]{:S(2)}) copy-start(s32[2304]{0:T(1024)} %param.14) | copy-start | bytes 27652

commit v5 on v3

--- a/solution.py
+++ b/solution.py
@@ -56,7 +56,7 @@
 
 N_Z, N_Q = 8, 8
 ORDER = (0, 7, 1, 6, 2, 5, 3, 4)
-PIECES = 3
+PIECES = 6
 
 
 def kernel(
@@ -295,9 +295,9 @@
     for step in range(4):
         for piece in range(PIECES):
             for way in range(2):
-                if step < 3 or (piece == 2) == way:
+                if step < 3 or (piece >= 3) == way:
                     hand_on(way, step, piece).wait_recv()
-                if step < 2 or (step == 2 and (piece == 2) == way):
+                if step < 2 or (step == 2 and (piece >= 3) == way):
                     hand_on(way, step + 1, piece).start()
         for way in range(2 if step < 3 else 1):
             pick(2 * step + 1 + way)
@@ -320,7 +320,7 @@
                 ring(ring_s.at[way * 4 + step], ring_r.at[way * 4 + step], rs_send, rs_recv, way, step, piece).wait_send()
         for step in range(4):
             for piece in range(PIECES):
-                if step < 3 or (piece == 2) == way:
+                if step < 3 or (piece >= 3) == way:
                     hand_on(way, step, piece).wait_send()
 
 

time: 67.7 us -> 67.7 us (level)
  no operation moved by 1% of the time
where the time goes in v5:
time: 67.7 us; the launch traced here: 67.6 us
  Pallas kernels  64.5 us (95%)
  local copies, waits for them, and re-layouts  2.45 us (4%)
    pallas_call x1, Pallas kernels, body(): pl.pallas_call(functools.partial(kernel, n_grp, n_dev), out_shape=(jax.Sh...  64.5 us
    unnamed x4, local copies, waits for them, and re-layouts  2.45 us

profile of v5, /device:TPU:1, one launch (start us, length us, event | category | flops | bytes accessed | tf_op | source)
XLA Modules:
  0.0 67.6 jit_solution(14130683469652989174)
XLA Ops:
  0.6 64.5 %sweep.1 = (bf16[384,512]{1,0:T(8,128)(2,1)}, bf16[96,512]{1,0:T(8,128)(2,1)}) custom-call(s32[18,128]{1,0:T(8,128)} %bitcast.3, s32[1,384]{1,0:T(1,128)} %bitcast.5, s32[3,128]{1,0:T(4,128)} %bitcast.4, bf16[384,512]{1,0:T(8,128)(2,1)} %nodes_ref.1, bf16[96,512]{1,0:T(8,128)(2,1)} %mids_ref.1, bf16[1024,512]{1,0:T(8,128)(2,1)} %w_ei.1, ...), custom_call_target="tpu_custom_call" | custom-call | flops 7000000000 | bytes 10000000 | tf_op jit(solution)/shard_map/sweep/pallas_call | solution.py:334
  65.1 0.0 copy-start
  65.1 1.8 %copy.17 = bf16[384,512]{1,0:T(8,128)(2,1)} copy(bf16[384,512]{1,0:T(8,128)(2,1)} %get-tuple-element.4) | data formatting | bytes 786432
  66.9 0.0 copy-done
  66.9 0.6 copy.18
Async XLA Ops:
  65.1 1.8 %copy-start = (bf16[96,512]{1,0:T(8,128)(2,1)S(1)}, bf16[96,512]{1,0:T(8,128)(2,1)}, u32[]{:S(2)}) copy-start(bf16[96,512]{1,0:T(8,128)(2,1)} %get-tuple-element.5) | copy-start | bytes 294916
